TPU v7x, 512 devices: a whole 4x4x16 slice. The times are simulated.
512 devices in a mesh: blk: 16 (over x_hi, y, core), wide: 32 (over x_lo, z).
Axes of the slice: x: 4 (x_hi: 2, x_lo: 2; x = x_hi * 2 + x_lo), y: 4, z: 16, core: 2. Of those that a mesh axis runs over, the one named last changes fastest.
Arguments:
- features: float32 [65536, 128], P(('blk', 'wide')), may hold values from -6 to 6
- inv_length: float32 [128], replicated, may hold values from 0.05 to 0.2
- vectors: float32 [8, 65536], P(None, ('blk', 'wide')), may hold values from -0.09375 to 0.09375
Outputs:
- product: float32 [8, 65536], P(None, ('blk', 'wide'))
All inputs are finite; a program needn't handle non-finite values.
Results may differ from a plain program's by a relative error of at most 0.0016.
Values may be sent and summed in bfloat16 or wider, within the bound.
A program may use at most 64 MiB of HBM per device.

v0:
```python
import jax
import jax.numpy as jnp
from jax import lax
from jax.sharding import PartitionSpec as P


def passed_along(value, axis, steps):
    count = lax.axis_size(axis)
    pairs = [(source, (source + steps) % count) for source in range(count)]
    return lax.ppermute(value, axis, pairs)


def kernel_tile(cols, rows, rows_norm):
    cols_norm = jnp.sum(jnp.square(cols.astype(jnp.float32)), axis=1)
    inner = lax.dot_general(
        cols, rows, (((1,), (1,)), ((), ())), preferred_element_type=jnp.float32
    )
    dist2 = jnp.maximum(cols_norm[:, None] + rows_norm[None, :] - 2.0 * inner, 0.0)
    scaled_r = jnp.sqrt(5.0 * dist2)
    return (1.0 + scaled_r + scaled_r * scaled_r / 3.0) * jnp.exp(-scaled_r)


def apply_tile(weights, tile):
    return jnp.dot(
        weights, tile, precision=lax.Precision.HIGHEST, preferred_element_type=jnp.float32
    )


def advance(cols, extra):
    wide_cols, extra = passed_along((cols.astype(jnp.float32), extra), "blk", 1)
    return (wide_cols.astype(jnp.bfloat16), extra)


def finish_block(accum):
    return lax.psum_scatter(accum, "wide", scatter_dimension=1, tiled=True)


def body(features, inv_length, vectors):
    scaled = (features * inv_length[None, :]).astype(jnp.bfloat16)
    block = lax.all_gather(scaled, "wide", axis=0, tiled=True)
    block_norm = jnp.sum(jnp.square(block.astype(jnp.float32)), axis=1)
    first = apply_tile(vectors, kernel_tile(scaled, block, block_norm))
    cycle_len = lax.axis_size("blk")

    def every_step(step, carry):
        cols, stacked, accum = carry
        cols, stacked = advance(cols, stacked)
        return (cols, stacked, accum + apply_tile(stacked[0], kernel_tile(cols, block, block_norm)))

    final = lax.fori_loop(1, cycle_len, every_step, (scaled, vectors[None], first))
    return finish_block(final[2])


def solution(mesh):
    return jax.shard_map(
        body,
        mesh=mesh,
        in_specs=(P(("blk", "wide"), None), P(), P(None, ("blk", "wide"))),
        out_specs=P(None, ("blk", "wide")),
        check_vma=False,
    )
```

profile of v0, /device:TPU:24, one launch (start us, length us, event | category | flops | bytes accessed | tf_op | source)
XLA Modules:
  0.0 483.3 jit_solution(6420223097096573364)
XLA Ops:
  8.8 136.7 %all-gather.2.cloned.1.call-done = bf16[4096,128]{1,0:T(8,128)(2,1)} async-done(((bf16[128,128]{1,0:T(8,128)(2,1)}), bf16[4096,128]{1,0:T(8,128)(2,1)}) %all-gather.2.cloned.1.call-update) | async-done | bytes 1048592 | tf_op jit(solution)/shard_map/all_gather | solution.py:40
  147.3 2.3 fusion.20
  151.3 196.2 %while.14 = (s32[]{:T(128)}, bf16[128,128]{1,0:T(8,128)(2,1)S(1)}, f32[1,8,128]{2,1,0:T(8,128)S(1)}, f32[8,4096]{1,0:T(8,128)S(1)}, f32[4096]{0:T(1024)S(1)}, /*index=5*/bf16[4096,128]{1,0:T(8,128)(2,1)S(1)}, s32[]{:T(128)}) while((s32[]{:T(128)}, bf16[128,128]{1,0:T(8,128)(2,1)S(1)}, f32[1,8,128]{2,1,0:T(8,128)S(1)}, ...), condition=%wide.region_4.0_spmd, body=%wide.region_2.0_spmd.sunk | while | flops 190398336 | bytes 5813405 | solution.py:50
  153.2 4.6 collective-permute-start.1
  161.5 2.2 collective-permute-start
  163.7 7.4 %collective-permute-start.1 = (f32[1,8,128]{2,1,0:T(8,128)S(1)}, f32[1,8,128]{2,1,0:T(8,128)S(1)}, u32[]{:S(2)}, u32[]{:S(2)}) collective-permute-start(f32[1,8,128]{2,1,0:T(8,128)S(1)} %get-tuple-element.98), channel_id=1, source_target_pairs={{0,32},{32,64},{64,96},{96,128},{128,160},{160,192},{192,224},{224... | collective-permute-start | bytes 12296 | tf_op jit(solution)/shard_map/while/body/eval_jaxpr/ppermute | solution.py:10
  174.8 2.2 collective-permute-start
  177.0 7.4 %collective-permute-start.1 = (f32[1,8,128]{2,1,0:T(8,128)S(1)}, f32[1,8,128]{2,1,0:T(8,128)S(1)}, u32[]{:S(2)}, u32[]{:S(2)}) collective-permute-start(f32[1,8,128]{2,1,0:T(8,128)S(1)} %get-tuple-element.98), channel_id=1, source_target_pairs={{0,32},{32,64},{64,96},{96,128},{128,160},{160,192},{192,224},{224... | collective-permute-start | bytes 12296 | tf_op jit(solution)/shard_map/while/body/eval_jaxpr/ppermute | solution.py:10
  188.0 2.2 collective-permute-start
  190.3 7.4 %collective-permute-start.1 = (f32[1,8,128]{2,1,0:T(8,128)S(1)}, f32[1,8,128]{2,1,0:T(8,128)S(1)}, u32[]{:S(2)}, u32[]{:S(2)}) collective-permute-start(f32[1,8,128]{2,1,0:T(8,128)S(1)} %get-tuple-element.98), channel_id=1, source_target_pairs={{0,32},{32,64},{64,96},{96,128},{128,160},{160,192},{192,224},{224... | collective-permute-start | bytes 12296 | tf_op jit(solution)/shard_map/while/body/eval_jaxpr/ppermute | solution.py:10
  201.3 2.2 collective-permute-start
  203.6 7.4 %collective-permute-start.1 = (f32[1,8,128]{2,1,0:T(8,128)S(1)}, f32[1,8,128]{2,1,0:T(8,128)S(1)}, u32[]{:S(2)}, u32[]{:S(2)}) collective-permute-start(f32[1,8,128]{2,1,0:T(8,128)S(1)} %get-tuple-element.98), channel_id=1, source_target_pairs={{0,32},{32,64},{64,96},{96,128},{128,160},{160,192},{192,224},{224... | collective-permute-start | bytes 12296 | tf_op jit(solution)/shard_map/while/body/eval_jaxpr/ppermute | solution.py:10
  214.6 2.2 collective-permute-start
  216.9 7.4 %collective-permute-start.1 = (f32[1,8,128]{2,1,0:T(8,128)S(1)}, f32[1,8,128]{2,1,0:T(8,128)S(1)}, u32[]{:S(2)}, u32[]{:S(2)}) collective-permute-start(f32[1,8,128]{2,1,0:T(8,128)S(1)} %get-tuple-element.98), channel_id=1, source_target_pairs={{0,32},{32,64},{64,96},{96,128},{128,160},{160,192},{192,224},{224... | collective-permute-start | bytes 12296 | tf_op jit(solution)/shard_map/while/body/eval_jaxpr/ppermute | solution.py:10
  230.2 7.4 %collective-permute-start.1 = (f32[1,8,128]{2,1,0:T(8,128)S(1)}, f32[1,8,128]{2,1,0:T(8,128)S(1)}, u32[]{:S(2)}, u32[]{:S(2)}) collective-permute-start(f32[1,8,128]{2,1,0:T(8,128)S(1)} %get-tuple-element.98), channel_id=1, source_target_pairs={{0,32},{32,64},{64,96},{96,128},{128,160},{160,192},{192,224},{224... | collective-permute-start | bytes 12296 | tf_op jit(solution)/shard_map/while/body/eval_jaxpr/ppermute | solution.py:10
  243.5 7.4 %collective-permute-start.1 = (f32[1,8,128]{2,1,0:T(8,128)S(1)}, f32[1,8,128]{2,1,0:T(8,128)S(1)}, u32[]{:S(2)}, u32[]{:S(2)}) collective-permute-start(f32[1,8,128]{2,1,0:T(8,128)S(1)} %get-tuple-element.98), channel_id=1, source_target_pairs={{0,32},{32,64},{64,96},{96,128},{128,160},{160,192},{192,224},{224... | collective-permute-start | bytes 12296 | tf_op jit(solution)/shard_map/while/body/eval_jaxpr/ppermute | solution.py:10
  256.7 7.4 %collective-permute-start.1 = (f32[1,8,128]{2,1,0:T(8,128)S(1)}, f32[1,8,128]{2,1,0:T(8,128)S(1)}, u32[]{:S(2)}, u32[]{:S(2)}) collective-permute-start(f32[1,8,128]{2,1,0:T(8,128)S(1)} %get-tuple-element.98), channel_id=1, source_target_pairs={{0,32},{32,64},{64,96},{96,128},{128,160},{160,192},{192,224},{224... | collective-permute-start | bytes 12296 | tf_op jit(solution)/shard_map/while/body/eval_jaxpr/ppermute | solution.py:10
  270.0 7.4 %collective-permute-start.1 = (f32[1,8,128]{2,1,0:T(8,128)S(1)}, f32[1,8,128]{2,1,0:T(8,128)S(1)}, u32[]{:S(2)}, u32[]{:S(2)}) collective-permute-start(f32[1,8,128]{2,1,0:T(8,128)S(1)} %get-tuple-element.98), channel_id=1, source_target_pairs={{0,32},{32,64},{64,96},{96,128},{128,160},{160,192},{192,224},{224... | collective-permute-start | bytes 12296 | tf_op jit(solution)/shard_map/while/body/eval_jaxpr/ppermute | solution.py:10
  283.3 7.4 %collective-permute-start.1 = (f32[1,8,128]{2,1,0:T(8,128)S(1)}, f32[1,8,128]{2,1,0:T(8,128)S(1)}, u32[]{:S(2)}, u32[]{:S(2)}) collective-permute-start(f32[1,8,128]{2,1,0:T(8,128)S(1)} %get-tuple-element.98), channel_id=1, source_target_pairs={{0,32},{32,64},{64,96},{96,128},{128,160},{160,192},{192,224},{224... | collective-permute-start | bytes 12296 | tf_op jit(solution)/shard_map/while/body/eval_jaxpr/ppermute | solution.py:10
  296.6 7.4 %collective-permute-start.1 = (f32[1,8,128]{2,1,0:T(8,128)S(1)}, f32[1,8,128]{2,1,0:T(8,128)S(1)}, u32[]{:S(2)}, u32[]{:S(2)}) collective-permute-start(f32[1,8,128]{2,1,0:T(8,128)S(1)} %get-tuple-element.98), channel_id=1, source_target_pairs={{0,32},{32,64},{64,96},{96,128},{128,160},{160,192},{192,224},{224... | collective-permute-start | bytes 12296 | tf_op jit(solution)/shard_map/while/body/eval_jaxpr/ppermute | solution.py:10
  309.9 7.4 %collective-permute-start.1 = (f32[1,8,128]{2,1,0:T(8,128)S(1)}, f32[1,8,128]{2,1,0:T(8,128)S(1)}, u32[]{:S(2)}, u32[]{:S(2)}) collective-permute-start(f32[1,8,128]{2,1,0:T(8,128)S(1)} %get-tuple-element.98), channel_id=1, source_target_pairs={{0,32},{32,64},{64,96},{96,128},{128,160},{160,192},{192,224},{224... | collective-permute-start | bytes 12296 | tf_op jit(solution)/shard_map/while/body/eval_jaxpr/ppermute | solution.py:10
  323.2 7.4 %collective-permute-start.1 = (f32[1,8,128]{2,1,0:T(8,128)S(1)}, f32[1,8,128]{2,1,0:T(8,128)S(1)}, u32[]{:S(2)}, u32[]{:S(2)}) collective-permute-start(f32[1,8,128]{2,1,0:T(8,128)S(1)} %get-tuple-element.98), channel_id=1, source_target_pairs={{0,32},{32,64},{64,96},{96,128},{128,160},{160,192},{192,224},{224... | collective-permute-start | bytes 12296 | tf_op jit(solution)/shard_map/while/body/eval_jaxpr/ppermute | solution.py:10
  336.5 7.4 %collective-permute-start.1 = (f32[1,8,128]{2,1,0:T(8,128)S(1)}, f32[1,8,128]{2,1,0:T(8,128)S(1)}, u32[]{:S(2)}, u32[]{:S(2)}) collective-permute-start(f32[1,8,128]{2,1,0:T(8,128)S(1)} %get-tuple-element.98), channel_id=1, source_target_pairs={{0,32},{32,64},{64,96},{96,128},{128,160},{160,192},{192,224},{224... | collective-permute-start | bytes 12296 | tf_op jit(solution)/shard_map/while/body/eval_jaxpr/ppermute | solution.py:10
  348.2 128.3 %reduce-scatter.2.cloned.1.call-done = f32[8,128]{1,0:T(8,128)} async-done(((f32[8,4096]{1,0:T(8,128)}), f32[8,128]{1,0:T(8,128)}) %reduce-scatter.2.cloned.1.call-update) | async-done | bytes 4112 | tf_op jit(solution)/shard_map/reduce_scatter | solution.py:35
  (129 shorter events, 82.2 us)
Async XLA Ops:
  6.5 138.9 %all-gather.2.cloned.1.call-start = ((), (), s32[]{:S(2)}) async-start(), calls=%async_computation.1 | async-start | bytes 1081344 | tf_op jit(solution)/shard_map/all_gather | solution.py:40
  8.7 467.8 %reduce-scatter.2.cloned.1.call-start = ((), (), s32[]{:S(2)}) async-start(), calls=%async_computation.2 | async-start | bytes 135168 | tf_op jit(solution)/shard_map/reduce_scatter | solution.py:35
  161.5 10.5 %collective-permute-start = (bf16[128,128]{1,0:T(8,128)(2,1)S(1)}, bf16[128,128]{1,0:T(8,128)(2,1)S(1)}, u32[]{:S(2)}, u32[]{:S(2)}) collective-permute-start(bf16[128,128]{1,0:T(8,128)(2,1)S(1)} %get-tuple-element.97), channel_id=1, source_target_pairs={{0,32},{32,64},{64,96},{96,128},{128,160},{160,192},{192,224},{224... | collective-permute-start | bytes 98312 | tf_op jit(solution)/shard_map/while/body/eval_jaxpr/ppermute | solution.py:10
  163.7 8.2 %collective-permute-start.1 = (f32[1,8,128]{2,1,0:T(8,128)S(1)}, f32[1,8,128]{2,1,0:T(8,128)S(1)}, u32[]{:S(2)}, u32[]{:S(2)}) collective-permute-start(f32[1,8,128]{2,1,0:T(8,128)S(1)} %get-tuple-element.98), channel_id=1, source_target_pairs={{0,32},{32,64},{64,96},{96,128},{128,160},{160,192},{192,224},{224... | collective-permute-start | bytes 12296 | tf_op jit(solution)/shard_map/while/body/eval_jaxpr/ppermute | solution.py:10
  174.8 10.5 %collective-permute-start = (bf16[128,128]{1,0:T(8,128)(2,1)S(1)}, bf16[128,128]{1,0:T(8,128)(2,1)S(1)}, u32[]{:S(2)}, u32[]{:S(2)}) collective-permute-start(bf16[128,128]{1,0:T(8,128)(2,1)S(1)} %get-tuple-element.97), channel_id=1, source_target_pairs={{0,32},{32,64},{64,96},{96,128},{128,160},{160,192},{192,224},{224... | collective-permute-start | bytes 98312 | tf_op jit(solution)/shard_map/while/body/eval_jaxpr/ppermute | solution.py:10
  177.0 8.2 %collective-permute-start.1 = (f32[1,8,128]{2,1,0:T(8,128)S(1)}, f32[1,8,128]{2,1,0:T(8,128)S(1)}, u32[]{:S(2)}, u32[]{:S(2)}) collective-permute-start(f32[1,8,128]{2,1,0:T(8,128)S(1)} %get-tuple-element.98), channel_id=1, source_target_pairs={{0,32},{32,64},{64,96},{96,128},{128,160},{160,192},{192,224},{224... | collective-permute-start | bytes 12296 | tf_op jit(solution)/shard_map/while/body/eval_jaxpr/ppermute | solution.py:10
  188.0 10.5 %collective-permute-start = (bf16[128,128]{1,0:T(8,128)(2,1)S(1)}, bf16[128,128]{1,0:T(8,128)(2,1)S(1)}, u32[]{:S(2)}, u32[]{:S(2)}) collective-permute-start(bf16[128,128]{1,0:T(8,128)(2,1)S(1)} %get-tuple-element.97), channel_id=1, source_target_pairs={{0,32},{32,64},{64,96},{96,128},{128,160},{160,192},{192,224},{224... | collective-permute-start | bytes 98312 | tf_op jit(solution)/shard_map/while/body/eval_jaxpr/ppermute | solution.py:10
  190.3 8.2 %collective-permute-start.1 = (f32[1,8,128]{2,1,0:T(8,128)S(1)}, f32[1,8,128]{2,1,0:T(8,128)S(1)}, u32[]{:S(2)}, u32[]{:S(2)}) collective-permute-start(f32[1,8,128]{2,1,0:T(8,128)S(1)} %get-tuple-element.98), channel_id=1, source_target_pairs={{0,32},{32,64},{64,96},{96,128},{128,160},{160,192},{192,224},{224... | collective-permute-start | bytes 12296 | tf_op jit(solution)/shard_map/while/body/eval_jaxpr/ppermute | solution.py:10
  201.3 10.5 %collective-permute-start = (bf16[128,128]{1,0:T(8,128)(2,1)S(1)}, bf16[128,128]{1,0:T(8,128)(2,1)S(1)}, u32[]{:S(2)}, u32[]{:S(2)}) collective-permute-start(bf16[128,128]{1,0:T(8,128)(2,1)S(1)} %get-tuple-element.97), channel_id=1, source_target_pairs={{0,32},{32,64},{64,96},{96,128},{128,160},{160,192},{192,224},{224... | collective-permute-start | bytes 98312 | tf_op jit(solution)/shard_map/while/body/eval_jaxpr/ppermute | solution.py:10
  203.6 8.2 %collective-permute-start.1 = (f32[1,8,128]{2,1,0:T(8,128)S(1)}, f32[1,8,128]{2,1,0:T(8,128)S(1)}, u32[]{:S(2)}, u32[]{:S(2)}) collective-permute-start(f32[1,8,128]{2,1,0:T(8,128)S(1)} %get-tuple-element.98), channel_id=1, source_target_pairs={{0,32},{32,64},{64,96},{96,128},{128,160},{160,192},{192,224},{224... | collective-permute-start | bytes 12296 | tf_op jit(solution)/shard_map/while/body/eval_jaxpr/ppermute | solution.py:10
  214.6 10.5 %collective-permute-start = (bf16[128,128]{1,0:T(8,128)(2,1)S(1)}, bf16[128,128]{1,0:T(8,128)(2,1)S(1)}, u32[]{:S(2)}, u32[]{:S(2)}) collective-permute-start(bf16[128,128]{1,0:T(8,128)(2,1)S(1)} %get-tuple-element.97), channel_id=1, source_target_pairs={{0,32},{32,64},{64,96},{96,128},{128,160},{160,192},{192,224},{224... | collective-permute-start | bytes 98312 | tf_op jit(solution)/shard_map/while/body/eval_jaxpr/ppermute | solution.py:10
  216.9 8.2 %collective-permute-start.1 = (f32[1,8,128]{2,1,0:T(8,128)S(1)}, f32[1,8,128]{2,1,0:T(8,128)S(1)}, u32[]{:S(2)}, u32[]{:S(2)}) collective-permute-start(f32[1,8,128]{2,1,0:T(8,128)S(1)} %get-tuple-element.98), channel_id=1, source_target_pairs={{0,32},{32,64},{64,96},{96,128},{128,160},{160,192},{192,224},{224... | collective-permute-start | bytes 12296 | tf_op jit(solution)/shard_map/while/body/eval_jaxpr/ppermute | solution.py:10
  227.9 10.5 %collective-permute-start = (bf16[128,128]{1,0:T(8,128)(2,1)S(1)}, bf16[128,128]{1,0:T(8,128)(2,1)S(1)}, u32[]{:S(2)}, u32[]{:S(2)}) collective-permute-start(bf16[128,128]{1,0:T(8,128)(2,1)S(1)} %get-tuple-element.97), channel_id=1, source_target_pairs={{0,32},{32,64},{64,96},{96,128},{128,160},{160,192},{192,224},{224... | collective-permute-start | bytes 98312 | tf_op jit(solution)/shard_map/while/body/eval_jaxpr/ppermute | solution.py:10
  230.2 8.2 %collective-permute-start.1 = (f32[1,8,128]{2,1,0:T(8,128)S(1)}, f32[1,8,128]{2,1,0:T(8,128)S(1)}, u32[]{:S(2)}, u32[]{:S(2)}) collective-permute-start(f32[1,8,128]{2,1,0:T(8,128)S(1)} %get-tuple-element.98), channel_id=1, source_target_pairs={{0,32},{32,64},{64,96},{96,128},{128,160},{160,192},{192,224},{224... | collective-permute-start | bytes 12296 | tf_op jit(solution)/shard_map/while/body/eval_jaxpr/ppermute | solution.py:10
  241.2 10.5 %collective-permute-start = (bf16[128,128]{1,0:T(8,128)(2,1)S(1)}, bf16[128,128]{1,0:T(8,128)(2,1)S(1)}, u32[]{:S(2)}, u32[]{:S(2)}) collective-permute-start(bf16[128,128]{1,0:T(8,128)(2,1)S(1)} %get-tuple-element.97), channel_id=1, source_target_pairs={{0,32},{32,64},{64,96},{96,128},{128,160},{160,192},{192,224},{224... | collective-permute-start | bytes 98312 | tf_op jit(solution)/shard_map/while/body/eval_jaxpr/ppermute | solution.py:10
  243.5 8.2 %collective-permute-start.1 = (f32[1,8,128]{2,1,0:T(8,128)S(1)}, f32[1,8,128]{2,1,0:T(8,128)S(1)}, u32[]{:S(2)}, u32[]{:S(2)}) collective-permute-start(f32[1,8,128]{2,1,0:T(8,128)S(1)} %get-tuple-element.98), channel_id=1, source_target_pairs={{0,32},{32,64},{64,96},{96,128},{128,160},{160,192},{192,224},{224... | collective-permute-start | bytes 12296 | tf_op jit(solution)/shard_map/while/body/eval_jaxpr/ppermute | solution.py:10
  254.5 10.5 %collective-permute-start = (bf16[128,128]{1,0:T(8,128)(2,1)S(1)}, bf16[128,128]{1,0:T(8,128)(2,1)S(1)}, u32[]{:S(2)}, u32[]{:S(2)}) collective-permute-start(bf16[128,128]{1,0:T(8,128)(2,1)S(1)} %get-tuple-element.97), channel_id=1, source_target_pairs={{0,32},{32,64},{64,96},{96,128},{128,160},{160,192},{192,224},{224... | collective-permute-start | bytes 98312 | tf_op jit(solution)/shard_map/while/body/eval_jaxpr/ppermute | solution.py:10
  267.8 10.5 %collective-permute-start = (bf16[128,128]{1,0:T(8,128)(2,1)S(1)}, bf16[128,128]{1,0:T(8,128)(2,1)S(1)}, u32[]{:S(2)}, u32[]{:S(2)}) collective-permute-start(bf16[128,128]{1,0:T(8,128)(2,1)S(1)} %get-tuple-element.97), channel_id=1, source_target_pairs={{0,32},{32,64},{64,96},{96,128},{128,160},{160,192},{192,224},{224... | collective-permute-start | bytes 98312 | tf_op jit(solution)/shard_map/while/body/eval_jaxpr/ppermute | solution.py:10
  270.0 8.2 %collective-permute-start.1 = (f32[1,8,128]{2,1,0:T(8,128)S(1)}, f32[1,8,128]{2,1,0:T(8,128)S(1)}, u32[]{:S(2)}, u32[]{:S(2)}) collective-permute-start(f32[1,8,128]{2,1,0:T(8,128)S(1)} %get-tuple-element.98), channel_id=1, source_target_pairs={{0,32},{32,64},{64,96},{96,128},{128,160},{160,192},{192,224},{224... | collective-permute-start | bytes 12296 | tf_op jit(solution)/shard_map/while/body/eval_jaxpr/ppermute | solution.py:10
  281.1 10.5 %collective-permute-start = (bf16[128,128]{1,0:T(8,128)(2,1)S(1)}, bf16[128,128]{1,0:T(8,128)(2,1)S(1)}, u32[]{:S(2)}, u32[]{:S(2)}) collective-permute-start(bf16[128,128]{1,0:T(8,128)(2,1)S(1)} %get-tuple-element.97), channel_id=1, source_target_pairs={{0,32},{32,64},{64,96},{96,128},{128,160},{160,192},{192,224},{224... | collective-permute-start | bytes 98312 | tf_op jit(solution)/shard_map/while/body/eval_jaxpr/ppermute | solution.py:10
  294.4 10.5 %collective-permute-start = (bf16[128,128]{1,0:T(8,128)(2,1)S(1)}, bf16[128,128]{1,0:T(8,128)(2,1)S(1)}, u32[]{:S(2)}, u32[]{:S(2)}) collective-permute-start(bf16[128,128]{1,0:T(8,128)(2,1)S(1)} %get-tuple-element.97), channel_id=1, source_target_pairs={{0,32},{32,64},{64,96},{96,128},{128,160},{160,192},{192,224},{224... | collective-permute-start | bytes 98312 | tf_op jit(solution)/shard_map/while/body/eval_jaxpr/ppermute | solution.py:10
  307.6 10.5 %collective-permute-start = (bf16[128,128]{1,0:T(8,128)(2,1)S(1)}, bf16[128,128]{1,0:T(8,128)(2,1)S(1)}, u32[]{:S(2)}, u32[]{:S(2)}) collective-permute-start(bf16[128,128]{1,0:T(8,128)(2,1)S(1)} %get-tuple-element.97), channel_id=1, source_target_pairs={{0,32},{32,64},{64,96},{96,128},{128,160},{160,192},{192,224},{224... | collective-permute-start | bytes 98312 | tf_op jit(solution)/shard_map/while/body/eval_jaxpr/ppermute | solution.py:10
  320.9 10.5 %collective-permute-start = (bf16[128,128]{1,0:T(8,128)(2,1)S(1)}, bf16[128,128]{1,0:T(8,128)(2,1)S(1)}, u32[]{:S(2)}, u32[]{:S(2)}) collective-permute-start(bf16[128,128]{1,0:T(8,128)(2,1)S(1)} %get-tuple-element.97), channel_id=1, source_target_pairs={{0,32},{32,64},{64,96},{96,128},{128,160},{160,192},{192,224},{224... | collective-permute-start | bytes 98312 | tf_op jit(solution)/shard_map/while/body/eval_jaxpr/ppermute | solution.py:10
  334.2 10.5 %collective-permute-start = (bf16[128,128]{1,0:T(8,128)(2,1)S(1)}, bf16[128,128]{1,0:T(8,128)(2,1)S(1)}, u32[]{:S(2)}, u32[]{:S(2)}) collective-permute-start(bf16[128,128]{1,0:T(8,128)(2,1)S(1)} %get-tuple-element.97), channel_id=1, source_target_pairs={{0,32},{32,64},{64,96},{96,128},{128,160},{160,192},{192,224},{224... | collective-permute-start | bytes 98312 | tf_op jit(solution)/shard_map/while/body/eval_jaxpr/ppermute | solution.py:10
  (11 other events, 66.0 us)
Sparse Core Ops, SparseCore 0:
  9.4 135.9 all-gather.1
  348.3 128.1 reduce-scatter.1
where the time goes:
time: 485 us; the launch traced here: 483 us
  waiting for transfers between devices  277 us (57%)
  starting transfers between devices  142 us (29%)
  matrix products  44 us (9%)
  between operations  13.5 us (3%)
    ppermute x30, starting transfers between devices, passed_along(): return lax.ppermute(value, axis, pairs)  142 us
    all_gather x1, waiting for transfers between devices, body(): block = lax.all_gather(scaled, 'wide', axis=0, tiled=True)  137 us
    reduce_scatter x1, waiting for transfers between devices, finish_block(): return lax.psum_scatter(accum, 'wide', scatter_dimension=1, tiled=True)  128 us
    dot_general x16, matrix products, apply_tile(): jnp.dot(weights, tile, precision=lax.Precision.HIGHEST, preferred_element...  26.2 us
    dot_general x16, matrix products, kernel_tile(): lax.dot_general(cols, rows, (((1,), (1,)), ((), ())), preferred_element_t...  17.8 us
    ppermute x30, waiting for transfers between devices, passed_along(): return lax.ppermute(value, axis, pairs)  12.1 us
  transfers between devices with their start and end apart: 32, of which 17 were waited for; matrix products, arithmetic and copies ran while one was open for 0% of the time, Pallas kernels for 0%

commit v1 on v0

v1 whole, which is shorter than its diff:
```python
import jax
import jax.numpy as jnp
from jax import lax
from jax.experimental import pallas as pl
from jax.experimental.pallas import tpu as pltpu
from jax.sharding import PartitionSpec as P

MESH = pl.DeviceIdType.MESH
F32, BF16 = jnp.float32, jnp.bfloat16

PTS = 128
FEAT = 128
RHS = 8
PLACES = 16
PLANES = 16
HALF = 8
HEAD = 2 * RHS
AUG = 16
ROWS = PLACES * PTS
PART = (HALF + 1) * PTS
COLS = 2 * PTS
CHUNK = 1024

SCALE = 5.0 / 3.0
ALPHA = 3.0 / 5.0**0.5
BETA = 0.6
DECAY = -(5.0**0.5) * 1.4426950408889634
TINY = 1e-30


def step_of(tile):
    return tile * (2 * (tile % 2) - 1) if isinstance(tile, int) else tile * (2 * lax.rem(tile, 2) - 1)


def split3(value):
    high = value.astype(BF16)
    rest = value - high.astype(F32)
    mid = rest.astype(BF16)
    low = (rest - mid.astype(F32)).astype(BF16)
    return high.astype(F32), mid.astype(F32), low.astype(F32)


def matern(dist2):
    dist2 = jnp.maximum(dist2, TINY)
    r = dist2 * lax.rsqrt(dist2)
    return ((r + ALPHA) * r + BETA) * jnp.exp2(r * DECAY)


def kernel(
    feat_ref, inv_ref, vec_ref, out_ref,
    abuf, bbuf, amat, va, vam, rowacc, corr, mean, cmsg, rmsg, rrecv, crecv,
    plane_send, plane_recv, line_send, line_recv, sib_send, sib_recv, row_send, row_recv, col_send, col_recv,
):
    blk, wide = lax.axis_index("blk"), lax.axis_index("wide")
    core = lax.rem(blk, 2)
    place = (2 * lax.div(blk, HALF) + lax.div(wide, PLANES)) * 4 + lax.rem(lax.div(blk, 2), 4)
    plane = lax.rem(wide, PLANES)

    def device(dz, dp, other):
        at = lax.rem(place + dp + PLACES, PLACES)
        x, y = lax.div(at, 4), lax.rem(at, 4)
        z = lax.rem(plane + dz + PLANES, PLANES)
        c = 1 - core if other else core
        return {"blk": lax.div(x, 2) * HALF + y * 2 + c, "wide": lax.rem(x, 2) * PLANES + z}

    def plane_copy(k):
        return pltpu.make_async_remote_copy(
            src_ref=abuf.at[0], dst_ref=abuf.at[k], send_sem=plane_send.at[k], recv_sem=plane_recv.at[k],
            device_id=device(0, -k, False), device_id_type=MESH,
        )

    def line_copy(tile):
        return pltpu.make_async_remote_copy(
            src_ref=bbuf.at[0, : HEAD + FEAT, :PTS], dst_ref=bbuf.at[tile, : HEAD + FEAT, :PTS],
            send_sem=line_send.at[tile], recv_sem=line_recv.at[tile],
            device_id=device(-step_of(tile), 0, False), device_id_type=MESH,
        )

    def sib_copy(tile):
        return pltpu.make_async_remote_copy(
            src_ref=bbuf.at[tile, : HEAD + FEAT, :PTS], dst_ref=bbuf.at[tile, : HEAD + FEAT, PTS:],
            send_sem=sib_send.at[tile], recv_sem=sib_recv.at[tile],
            device_id=device(0, 0, True), device_id_type=MESH,
        )

    def row_copy(k):
        return pltpu.make_async_remote_copy(
            src_ref=rmsg.at[k], dst_ref=rrecv.at[k], send_sem=row_send.at[k], recv_sem=row_recv.at[k],
            device_id=device(0, k, False), device_id_type=MESH,
        )

    def col_copy(tile, other):
        return pltpu.make_async_remote_copy(
            src_ref=cmsg.at[tile, other], dst_ref=crecv.at[tile, other],
            send_sem=col_send.at[tile, other], recv_sem=col_recv.at[tile, other],
            device_id=device(step_of(tile), 0, other == 1), device_id_type=MESH,
        )

    barrier = pltpu.get_barrier_semaphore()
    for k in range(1, PLACES):
        pl.semaphore_signal(barrier, inc=1, device_id=device(0, k, False), device_id_type=MESH)
    for tile in range(1, HALF + 1):
        pl.semaphore_signal(barrier, inc=1, device_id=device(step_of(tile), 0, False), device_id_type=MESH)
    pl.semaphore_signal(barrier, inc=1, device_id=device(0, 0, True), device_id_type=MESH)

    scaled = (feat_ref[...] * inv_ref[...]).astype(BF16).astype(F32)
    vec = vec_ref[...]
    vec_high = vec.astype(BF16).astype(F32)
    head = jnp.concatenate([vec_high, vec - vec_high], axis=0).astype(BF16)
    abuf[0, :PTS, :] = (scaled * -2.0).astype(BF16)
    abuf[0, PTS:, :] = head
    bbuf[0, :HEAD, :PTS] = head
    bbuf[0, HEAD : HEAD + FEAT, :PTS] = scaled.T.astype(BF16)

    pl.semaphore_wait(barrier, PLACES - 1 + HALF + 1)

    sib_copy(0).start()
    for tile in range(1, HALF + 1):
        line_copy(tile).start()
    for k in range(1, PLACES):
        plane_copy(k).start()

    lane = lax.broadcasted_iota(jnp.int32, (PTS, PTS), 1)
    ones = jnp.ones((2 * FEAT, PTS), BF16)

    def add_rows(k):
        at = pl.multiple_of(k * PTS, PTS)
        points = abuf[k, :PTS, :]
        wide_points = points.astype(F32)
        square = wide_points * wide_points
        high = square.astype(BF16)
        low = (square - high.astype(F32)).astype(BF16)
        norm = 0.25 * jnp.dot(jnp.concatenate([high, low], axis=1), ones, preferred_element_type=F32)
        n0, n1, n2 = split3(norm)
        extra = jnp.where(lane == 0, n0, jnp.where(lane == 1, n1, jnp.where(lane == 2, n2, jnp.where(lane < 6, 1.0, 0.0))))
        amat[pl.ds(at, PTS), :FEAT] = points
        amat[pl.ds(at, PTS), FEAT:] = extra.astype(BF16)
        va[:, pl.ds(at, PTS)] = abuf[k, PTS:, :]

    add_rows(0)

    def arrive(k, _):
        plane_copy(k).wait_recv()
        add_rows(k)
        return 0

    lax.fori_loop(1, PLACES, arrive, 0)

    k_of = lax.div(lax.broadcasted_iota(jnp.int32, (HEAD, PART), 1), PTS)
    vam[...] = jnp.where((k_of > 0) & (k_of < HALF), va[:, :PART].astype(F32), 0.0).astype(BF16)
    mean[...] = (jnp.dot(jnp.full((HEAD, ROWS), 1.0 / ROWS, BF16), amat[...], preferred_element_type=F32)).astype(BF16)

    def both(value):
        return value[:RHS] + value[RHS:]

    sum_full = jnp.sum(both(va[...].astype(F32)), axis=1, keepdims=True)
    sum_part = jnp.sum(both(vam[...].astype(F32)), axis=1, keepdims=True)
    rowacc[...] = jnp.zeros_like(rowacc)
    corr[...] = jnp.zeros_like(corr)

    sub = lax.broadcasted_iota(jnp.int32, (AUG, COLS), 0)

    def run_tile(tile, rows, weights, weight_sum, which):
        cols = bbuf[tile, HEAD : HEAD + FEAT, :].astype(F32)
        n0, n1, n2 = split3(jnp.sum(cols * cols, axis=0, keepdims=True))
        extra = jnp.where(sub < 3, 1.0, jnp.where(sub == 3, n0, jnp.where(sub == 4, n1, jnp.where(sub == 5, n2, 0.0))))
        bbuf[tile, HEAD + FEAT :, :] = extra.astype(BF16)
        right = bbuf[tile, HEAD:, :]
        vb = bbuf[tile, :HEAD, :]
        middle = matern(jnp.dot(mean[:, : FEAT + AUG], right, preferred_element_type=F32)[:RHS])
        vb_wide = vb.astype(F32)
        corr[which] += both(vb_wide) * middle
        col = weight_sum * middle
        start = 0
        while start < rows:
            size = min(CHUNK, rows - start)
            if rows - start - size < CHUNK // 2:
                size = rows - start
            dist2 = jnp.dot(amat[start : start + size, : FEAT + AUG], right, preferred_element_type=F32)
            entry = matern(dist2).reshape(size // RHS, RHS, COLS) - middle[None]
            entry = entry.reshape(size, COLS).astype(BF16)
            rowacc[:, start : start + size] += lax.dot_general(
                vb, entry, (((1,), (1,)), ((), ())), preferred_element_type=F32
            )
            col += both(jnp.dot(weights[:, start : start + size], entry, preferred_element_type=F32))
            start += size
        cmsg[tile, 0] = col[:, :PTS]
        cmsg[tile, 1] = col[:, PTS:]

    line_copy(1).wait_recv()
    sib_copy(1).start()

    def full_tile(tile, _):
        line_copy(tile + 1).wait_recv()
        sib_copy(tile + 1).start()
        sib_copy(tile).wait_recv()
        run_tile(tile, ROWS, va, sum_full, 0)
        col_copy(tile, 0).start()
        col_copy(tile, 1).start()
        return 0

    lax.fori_loop(1, HALF, full_tile, 0)

    const_full = jnp.sum(corr[0], axis=1, keepdims=True)

    for k in range(HALF + 1, PLACES):
        rmsg[k] = both(rowacc[:, k * PTS : (k + 1) * PTS]) + const_full
        row_copy(k).start()

    sib_copy(HALF).wait_recv()
    run_tile(HALF, PART, vam, sum_part, 1)
    col_copy(HALF, 0).start()
    col_copy(HALF, 1).start()

    sib_copy(0).wait_recv()
    run_tile(0, PART, vam, sum_part, 1)
    col_copy(0, 1).start()

    const_part = const_full + jnp.sum(corr[1], axis=1, keepdims=True)
    for k in range(1, HALF + 1):
        rmsg[k] = both(rowacc[:, k * PTS : (k + 1) * PTS]) + const_part
        row_copy(k).start()

    total = both(rowacc[:, :PTS]) + const_part + cmsg[0, 0]
    for tile in range(HALF + 1):
        for other in range(2):
            if tile or other:
                col_copy(tile, other).wait_recv()
                total += crecv[tile, other]
    for k in list(range(HALF + 1, PLACES)) + list(range(1, HALF + 1)):
        row_copy(k).wait_recv()
        total += rrecv[k]
    out_ref[...] = total * SCALE

    for tile in range(HALF + 1):
        sib_copy(tile).wait_send()
        if tile:
            line_copy(tile).wait_send()
            col_copy(tile, 0).wait_send()
        col_copy(tile, 1).wait_send()
    for k in range(1, PLACES):
        plane_copy(k).wait_send()
        row_copy(k).wait_send()


def body(features, inv_length, vectors):
    dma = pltpu.SemaphoreType.DMA
    return pl.pallas_call(
        kernel,
        out_shape=jax.ShapeDtypeStruct((RHS, PTS), F32),
        in_specs=[pl.BlockSpec(memory_space=pltpu.VMEM)] * 3,
        out_specs=pl.BlockSpec(memory_space=pltpu.VMEM),
        scratch_shapes=[
            pltpu.VMEM((PLACES, PTS + HEAD, FEAT), BF16),
            pltpu.VMEM((HALF + 1, HEAD + FEAT + AUG, COLS), BF16),
            pltpu.VMEM((ROWS, 2 * FEAT), BF16),
            pltpu.VMEM((HEAD, ROWS), BF16),
            pltpu.VMEM((HEAD, PART), BF16),
            pltpu.VMEM((HEAD, ROWS), F32),
            pltpu.VMEM((2, RHS, COLS), F32),
            pltpu.VMEM((HEAD, 2 * FEAT), BF16),
            pltpu.VMEM((HALF + 1, 2, RHS, PTS), F32),
            pltpu.VMEM((PLACES, RHS, PTS), F32),
            pltpu.VMEM((PLACES, RHS, PTS), F32),
            pltpu.VMEM((HALF + 1, 2, RHS, PTS), F32),
            dma((PLACES,)), dma((PLACES,)),
            dma((HALF + 1,)), dma((HALF + 1,)),
            dma((HALF + 1,)), dma((HALF + 1,)),
            dma((PLACES,)), dma((PLACES,)),
            dma((HALF + 1, 2)), dma((HALF + 1, 2)),
        ],
        compiler_params=pltpu.CompilerParams(
            collective_id=0, has_side_effects=True, vmem_limit_bytes=48 * 2**20
        ),
        name="matern",
    )(features, inv_length.reshape(1, FEAT), vectors)


def solution(mesh):
    return jax.shard_map(
        body,
        mesh=mesh,
        in_specs=(P(("blk", "wide"), None), P(), P(None, ("blk", "wide"))),
        out_specs=P(None, ("blk", "wide")),
        check_vma=False,
    )
```

time: 485 us -> 50.3 us (0.10)
  the two profiles are of different devices: /device:TPU:24 before, /device:TPU:1 now
where the time goes in v1:
time: 50.3 us; the launch traced here: 50.1 us
  Pallas kernels  47.3 us (94%)
  local copies, waits for them, and re-layouts  2.78 us (6%)
    pallas_call x1, Pallas kernels, body(): pl.pallas_call(kernel, out_shape=jax.ShapeDtypeStruct((RHS, PTS), F32), i...  47.3 us
    unnamed x7, local copies, waits for them, and re-layouts  2.78 us

profile of v1, /device:TPU:1, one launch (start us, length us, event | category | flops | bytes accessed | tf_op | source)
XLA Modules:
  0.0 50.1 jit_solution(14146066473549036615)
XLA Ops:
  0.0 0.0 copy-start.2
  0.0 0.7 %copy-done.2 = f32[128]{0:T(128)S(1)} copy-done((f32[128]{0:T(128)S(1)}, f32[128]{0:T(128)}, u32[]{:S(2)}) %copy-start.2) | copy-done | bytes 536
  0.7 0.0 copy-start
  0.7 0.8 %copy-done = f32[128,128]{1,0:T(8,128)S(1)} copy-done((f32[128,128]{1,0:T(8,128)S(1)}, f32[128,128]{1,0:T(8,128)}, u32[]{:S(2)}) %copy-start) | copy-done | bytes 65560
  1.5 0.0 copy-start.1
  1.5 0.7 %copy-done.1 = f32[8,128]{1,0:T(8,128)S(1)} copy-done((f32[8,128]{1,0:T(8,128)S(1)}, f32[8,128]{1,0:T(8,128)}, u32[]{:S(2)}) %copy-start.1) | copy-done | bytes 4120
  2.2 47.3 %matern.1 = f32[8,128]{1,0:T(8,128)S(1)} custom-call(f32[128,128]{1,0:T(8,128)S(1)} %copy-done, f32[1,128]{1,0:T(1,128)S(1)} %bitcast.1, f32[8,128]{1,0:T(8,128)S(1)} %copy-done.1), custom_call_target="tpu_custom_call" | custom-call | tf_op jit(solution)/shard_map/matern/pallas_call | solution.py:248
  49.5 0.6 %copy.5 = f32[8,128]{1,0:T(8,128)} copy(f32[8,128]{1,0:T(8,128)S(1)} %matern.1) | data formatting | bytes 8192
Async XLA Ops:
  0.0 0.7 %copy-start.2 = (f32[128]{0:T(128)S(1)}, f32[128]{0:T(128)}, u32[]{:S(2)}) copy-start(f32[128]{0:T(128)} %param.4) | copy-start | bytes 1540
  0.7 0.8 %copy-start = (f32[128,128]{1,0:T(8,128)S(1)}, f32[128,128]{1,0:T(8,128)}, u32[]{:S(2)}) copy-start(f32[128,128]{1,0:T(8,128)} %feat_ref.1) | copy-start | bytes 196612
  1.5 0.7 %copy-start.1 = (f32[8,128]{1,0:T(8,128)S(1)}, f32[8,128]{1,0:T(8,128)}, u32[]{:S(2)}) copy-start(f32[8,128]{1,0:T(8,128)} %vec_ref.1) | copy-start | bytes 12292

commit v2 on v1

v2 whole, which is shorter than its diff:
```python
import jax
import jax.numpy as jnp
from jax import lax
from jax.experimental import pallas as pl
from jax.experimental.pallas import tpu as pltpu
from jax.sharding import PartitionSpec as P

MESH = pl.DeviceIdType.MESH
F32, BF16 = jnp.float32, jnp.bfloat16

PTS = 128
FEAT = 128
RHS = 8
PLACES = 16
PLANES = 16
HALF = 8
HEAD = 2 * RHS
AUG = 16
ROWS = PLACES * PTS
PART = (HALF + 1) * PTS
COLS = 2 * PTS
NEAR_LAST = (10, 6, 9, 7, 11, 5, 14, 2, 8, 13, 3, 15, 1, 12, 4)
RELAY = 6

SCALE = 5.0 / 3.0
ALPHA = 3.0 / 5.0**0.5
BETA = 0.6
DECAY = -(5.0**0.5) * 1.4426950408889634
TINY = 1e-30


def packed(*tiles):
    return sum((tile - 1) * 8**i for i, tile in enumerate(tiles))


ORDERS = (packed(1, 2, 3, 4, 6, 5, 7, 8), packed(6, 8, 7, 5, 1, 2, 3, 4), packed(4, 3, 1, 2, 8, 7, 6, 5))


def step_of(tile):
    return tile * (1 - 2 * ((tile + 3) // 8))


def split3(value):
    high = value.astype(BF16)
    rest = value - high.astype(F32)
    mid = rest.astype(BF16)
    low = (rest - mid.astype(F32)).astype(BF16)
    return high.astype(F32), mid.astype(F32), low.astype(F32)


def matern(dist2):
    dist2 = jnp.maximum(dist2, TINY)
    r = dist2 * lax.rsqrt(dist2)
    return ((r + ALPHA) * r + BETA) * jnp.exp2(r * DECAY)


def kernel(
    feat_hbm, inv_hbm, vec_hbm, out_ref,
    feat_ref, inv_ref, vec_ref, abuf, bbuf, amat, va, rowacc, corr, mean, mid, wsum, colacc, cmsg, rmsg, rrecv, crecv,
    in_sem, plane_send, plane_recv, line_send, line_recv, sib_send, sib_recv, row_send, row_recv, col_send, col_recv,
):
    loads = [
        pltpu.make_async_copy(src, dst, in_sem.at[i])
        for i, (src, dst) in enumerate(((feat_hbm, feat_ref), (inv_hbm, inv_ref), (vec_hbm, vec_ref)))
    ]
    for load in loads:
        load.start()

    blk, wide = lax.axis_index("blk"), lax.axis_index("wide")
    core = lax.rem(blk, 2)
    place = (2 * lax.div(blk, HALF) + lax.div(wide, PLANES)) * 4 + lax.rem(lax.div(blk, 2), 4)
    plane = lax.rem(wide, PLANES)

    def device(dz, dp, other):
        at = lax.rem(place + dp + PLACES, PLACES)
        x, y = lax.div(at, 4), lax.rem(at, 4)
        z = lax.rem(plane + dz + PLANES, PLANES)
        c = 1 - core if other else core
        return {"blk": lax.div(x, 2) * HALF + y * 2 + c, "wide": lax.rem(x, 2) * PLANES + z}

    def plane_copy(k):
        return pltpu.make_async_remote_copy(
            src_ref=abuf.at[0], dst_ref=abuf.at[k], send_sem=plane_send.at[k], recv_sem=plane_recv.at[k],
            device_id=device(0, -k, False), device_id_type=MESH,
        )

    def line_copy(tile, source=0, hops=0):
        return pltpu.make_async_remote_copy(
            src_ref=bbuf.at[source, : HEAD + FEAT, :PTS], dst_ref=bbuf.at[tile, : HEAD + FEAT, :PTS],
            send_sem=line_send.at[tile], recv_sem=line_recv.at[tile],
            device_id=device(hops, 0, False), device_id_type=MESH,
        )

    def sib_copy(tile):
        return pltpu.make_async_remote_copy(
            src_ref=bbuf.at[tile, : HEAD + FEAT, :PTS], dst_ref=bbuf.at[tile, : HEAD + FEAT, PTS:],
            send_sem=sib_send.at[tile], recv_sem=sib_recv.at[tile],
            device_id=device(0, 0, True), device_id_type=MESH,
        )

    def row_copy(k):
        return pltpu.make_async_remote_copy(
            src_ref=rmsg.at[k], dst_ref=rrecv.at[k], send_sem=row_send.at[k], recv_sem=row_recv.at[k],
            device_id=device(0, k, False), device_id_type=MESH,
        )

    def col_copy(tile, other):
        return pltpu.make_async_remote_copy(
            src_ref=cmsg.at[tile, other], dst_ref=crecv.at[tile, other],
            send_sem=col_send.at[tile, other], recv_sem=col_recv.at[tile, other],
            device_id=device(step_of(tile), 0, other == 1), device_id_type=MESH,
        )

    barrier = pltpu.get_barrier_semaphore()
    for dz in (-RELAY, 2, -2, 1, -1):
        pl.semaphore_signal(barrier, inc=1, device_id=device(dz, 0, False), device_id_type=MESH)
    for k in NEAR_LAST:
        pl.semaphore_signal(barrier, inc=1, device_id=device(0, k, False), device_id_type=MESH)
    pl.semaphore_signal(barrier, inc=1, device_id=device(0, 0, True), device_id_type=MESH)

    for load in loads:
        load.wait()
    scaled = (feat_ref[...] * inv_ref[...]).astype(BF16).astype(F32)
    vec = vec_ref[...]
    vec_high = vec.astype(BF16).astype(F32)
    head = jnp.concatenate([vec_high, vec - vec_high], axis=0).astype(BF16)
    abuf[0, :PTS, :] = (scaled * -2.0).astype(BF16)
    abuf[0, PTS:, :] = head
    bbuf[0, :HEAD, :PTS] = head
    bbuf[0, HEAD : HEAD + FEAT, :PTS] = scaled.T.astype(BF16)

    pl.semaphore_wait(barrier, PLACES - 1 + 5 + 1)

    line_copy(RELAY, 0, RELAY).start()
    line_copy(2, 0, -2).start()
    line_copy(1, 0, -1).start()
    sib_copy(0).start()
    for k in range(1, PLACES):
        plane_copy(k).start()

    lane = lax.broadcasted_iota(jnp.int32, (PTS, PTS), 1)
    ones = jnp.ones((2 * FEAT, PTS), BF16)

    def add_rows(k):
        at = pl.multiple_of(k * PTS, PTS)
        points = abuf[k, :PTS, :]
        wide_points = points.astype(F32)
        square = wide_points * wide_points
        high = square.astype(BF16)
        low = (square - high.astype(F32)).astype(BF16)
        norm = 0.25 * jnp.dot(jnp.concatenate([high, low], axis=1), ones, preferred_element_type=F32)
        n0, n1, n2 = split3(norm)
        extra = jnp.where(lane == 0, n0, jnp.where(lane == 1, n1, jnp.where(lane == 2, n2, jnp.where(lane < 6, 1.0, 0.0))))
        amat[pl.ds(at, PTS), :FEAT] = points
        amat[pl.ds(at, PTS), FEAT:] = extra.astype(BF16)
        va[0, :, pl.ds(at, PTS)] = abuf[k, PTS:, :]

    def arrive(k, _):
        plane_copy(k).wait_recv()
        add_rows(k)
        return 0

    add_rows(0)
    rowacc[...] = jnp.zeros_like(rowacc)
    corr[...] = jnp.zeros_like(corr)
    lax.fori_loop(1, 5, arrive, 0)
    line_copy(1).wait_recv()
    sib_copy(1).start()
    line_copy(2).wait_recv()
    line_copy(4, 2, -2).start()
    line_copy(3, 2, -1).start()
    sib_copy(2).start()
    lax.fori_loop(5, HALF + 1, arrive, 0)

    def both(value):
        return value[:RHS] + value[RHS:]

    k_of = lax.div(lax.broadcasted_iota(jnp.int32, (HEAD, PART), 1), PTS)
    masked = jnp.where((k_of > 0) & (k_of < HALF), va[0, :, :PART].astype(F32), 0.0)
    va[1, :, :PART] = masked.astype(BF16)

    def spread(value):
        return jnp.broadcast_to(jnp.sum(both(value), axis=1, keepdims=True), (RHS, COLS))

    wsum[0] = spread(va[0, :, :PART].astype(F32))
    wsum[1] = spread(masked)
    mean[...] = jnp.dot(jnp.full((HEAD, PART), 1.0 / PART, BF16), amat[:PART], preferred_element_type=F32).astype(BF16)

    sub = lax.broadcasted_iota(jnp.int32, (AUG, COLS), 0)

    def add_columns(tile):
        cols = bbuf[tile, HEAD : HEAD + FEAT, :].astype(F32)
        n0, n1, n2 = split3(jnp.sum(cols * cols, axis=0, keepdims=True))
        extra = jnp.where(sub < 3, 1.0, jnp.where(sub == 3, n0, jnp.where(sub == 4, n1, jnp.where(sub == 5, n2, 0.0))))
        bbuf[tile, HEAD + FEAT :, :] = extra.astype(BF16)
        mid[tile] = matern(jnp.dot(mean[:, : FEAT + AUG], bbuf[tile, HEAD:, :], preferred_element_type=F32)[:RHS])

    def run_part(tile, first, last, weights):
        middle = mid[tile]
        vb = bbuf[tile, :HEAD, :]
        if first == 0:
            corr[0] += both(vb.astype(F32)) * middle
        if last == ROWS:
            corr[1] += both(vb.astype(F32)) * middle
        dist2 = jnp.dot(amat[first:last, : FEAT + AUG], bbuf[tile, HEAD:, :], preferred_element_type=F32)
        entry = matern(dist2).reshape((last - first) // RHS, RHS, COLS) - middle[None]
        entry = entry.reshape(last - first, COLS).astype(BF16)
        rowacc[:, first:last] += lax.dot_general(vb, entry, (((1,), (1,)), ((), ())), preferred_element_type=F32)
        return both(jnp.dot(weights, entry, preferred_element_type=F32))

    def first_part(tile):
        kind = (HALF - lax.rem(tile, HALF)) // HALF
        add_columns(tile)
        colacc[tile] = run_part(tile, 0, PART, va[kind, :, :PART]) + wsum[kind] * mid[tile]

    def second_part(tile):
        colacc[tile] += run_part(tile, PART, ROWS, va[0, :, PART:]) + wsum[2] * mid[tile]

    def whole_tile(tile):
        add_columns(tile)
        colacc[tile] = run_part(tile, 0, ROWS, va[0]) + (wsum[0] + wsum[2]) * mid[tile]

    def send_columns(tile):
        total = colacc[tile]
        cmsg[tile, 0] = total[:, :PTS]
        cmsg[tile, 1] = total[:, PTS:]
        col_copy(tile, 0).start()
        col_copy(tile, 1).start()

    def send_rows(ks, part):
        const = jnp.sum(corr[part], axis=1, keepdims=True)
        for k in ks:
            rmsg[k] = both(rowacc[:, k * PTS : (k + 1) * PTS]) + const
            if k:
                row_copy(k).start()

    def fetch(tile):
        line_copy(tile).wait_recv()
        sib_copy(tile).start()

    def slot(index, order):
        late = index > 2
        tile = lax.select(late, lax.rem(order, 8) + 1, index)
        order = lax.select(late, order // 8, order)
        after = lax.rem(order, 8) + 1

        @pl.when(index == 1)
        def _():
            line_copy(RELAY).wait_recv()
            line_copy(8, RELAY, 2).start()
            line_copy(7, RELAY, 1).start()
            line_copy(5, RELAY, -1).start()
            sib_copy(RELAY).start()

        @pl.when(index == 3)
        def _():
            lax.fori_loop(HALF + 1, PLACES, arrive, 0)
            wsum[2] = spread(va[0, :, PART:].astype(F32))

        @pl.when((index > 1) & (index < 10) & (after > 2) & (after != RELAY))
        def _():
            fetch(after)

        @pl.when((index < 3) | (tile > 2))
        def _():
            sib_copy(tile).wait_recv()

        @pl.when((index < 3) | (tile == HALF))
        def _():
            first_part(tile)

        @pl.when(late & (tile < 3))
        def _():
            second_part(tile)

        @pl.when(late & (tile > 2) & (tile < HALF))
        def _():
            whole_tile(tile)

        @pl.when(late)
        def _():
            send_columns(tile)

        return order

    third, quarter = lax.div(plane, 8), lax.div(plane, 12)
    order = ORDERS[0] + third * (ORDERS[1] - ORDERS[0]) + quarter * (ORDERS[2] - ORDERS[1])
    lax.fori_loop(0, 11, slot, order)

    send_rows(range(HALF + 1), 0)
    send_rows(range(HALF + 1, PLACES), 1)
    cmsg[0, 1] = colacc[0, :, PTS:]
    col_copy(0, 1).start()

    total = rmsg[0] + colacc[0, :, :PTS]
    for tile in range(HALF + 1):
        for other in range(2):
            if tile or other:
                col_copy(tile, other).wait_recv()
                total += crecv[tile, other]
    for k in range(1, PLACES):
        row_copy(k).wait_recv()
        total += rrecv[k]
    out_ref[...] = total * SCALE

    for tile in range(HALF + 1):
        sib_copy(tile).wait_send()
        if tile:
            line_copy(tile).wait_send()
            col_copy(tile, 0).wait_send()
        col_copy(tile, 1).wait_send()
    for k in range(1, PLACES):
        plane_copy(k).wait_send()
        row_copy(k).wait_send()


def body(features, inv_length, vectors):
    dma = pltpu.SemaphoreType.DMA
    return pl.pallas_call(
        kernel,
        out_shape=jax.ShapeDtypeStruct((RHS, PTS), F32),
        in_specs=[pl.BlockSpec(memory_space=pltpu.HBM)] * 3,
        out_specs=pl.BlockSpec(memory_space=pltpu.VMEM),
        scratch_shapes=[
            pltpu.VMEM((PTS, FEAT), F32),
            pltpu.VMEM((1, FEAT), F32),
            pltpu.VMEM((RHS, PTS), F32),
            pltpu.VMEM((PLACES, PTS + HEAD, FEAT), BF16),
            pltpu.VMEM((HALF + 1, HEAD + FEAT + AUG, COLS), BF16),
            pltpu.VMEM((ROWS, 2 * FEAT), BF16),
            pltpu.VMEM((2, HEAD, ROWS), BF16),
            pltpu.VMEM((HEAD, ROWS), F32),
            pltpu.VMEM((2, RHS, COLS), F32),
            pltpu.VMEM((HEAD, 2 * FEAT), BF16),
            pltpu.VMEM((HALF + 1, RHS, COLS), F32),
            pltpu.VMEM((3, RHS, COLS), F32),
            pltpu.VMEM((HALF + 1, RHS, COLS), F32),
            pltpu.VMEM((HALF + 1, 2, RHS, PTS), F32),
            pltpu.VMEM((PLACES, RHS, PTS), F32),
            pltpu.VMEM((PLACES, RHS, PTS), F32),
            pltpu.VMEM((HALF + 1, 2, RHS, PTS), F32),
            dma((3,)),
            dma((PLACES,)), dma((PLACES,)),
            dma((HALF + 1,)), dma((HALF + 1,)),
            dma((HALF + 1,)), dma((HALF + 1,)),
            dma((PLACES,)), dma((PLACES,)),
            dma((HALF + 1, 2)), dma((HALF + 1, 2)),
        ],
        compiler_params=pltpu.CompilerParams(
            collective_id=0, has_side_effects=True, vmem_limit_bytes=60 * 2**20
        ),
        name="matern",
    )(features, inv_length.reshape(1, FEAT), vectors)


def solution(mesh):
    return jax.shard_map(
        body,
        mesh=mesh,
        in_specs=(P(("blk", "wide"), None), P(), P(None, ("blk", "wide"))),
        out_specs=P(None, ("blk", "wide")),
        check_vma=False,
    )
```

time: 50.3 us -> 45 us (0.89)
  Pallas kernels: 47.3 us -> 43.5 us
  local copies, waits for them, and re-layouts: 2.78 us -> 1.28 us
    pallas_call x1, Pallas kernels: 47.3 us -> 43.5 us  [body(): pl.pallas_call(kernel, out_shape=jax.ShapeDtypeStruct((RHS, PTS), F32), i...]
    unnamed x7 -> x1, local copies, waits for them, and re-layouts: 2.78 us -> 1.28 us
where the time goes in v2:
time: 45 us; the launch traced here: 44.8 us
  Pallas kernels  43.5 us (97%)
  local copies, waits for them, and re-layouts  1.28 us (3%)
    pallas_call x1, Pallas kernels, body(): pl.pallas_call(kernel, out_shape=jax.ShapeDtypeStruct((RHS, PTS), F32), i...  43.5 us
    unnamed x1, local copies, waits for them, and re-layouts  1.28 us

profile of v2, /device:TPU:1, one launch (start us, length us, event | category | flops | bytes accessed | tf_op | source)
XLA Modules:
  0.0 44.8 jit_solution(1801534189957913911)
XLA Ops:
  0.0 43.5 %matern.1 = f32[8,128]{1,0:T(8,128)} custom-call(f32[128,128]{1,0:T(8,128)} %feat_hbm.1, f32[1,128]{1,0:T(1,128)} %bitcast.1, f32[8,128]{1,0:T(8,128)} %vec_hbm.1), custom_call_target="tpu_custom_call" | custom-call | tf_op jit(solution)/shard_map/matern/pallas_call | solution.py:319
  43.5 1.3 %copy.5 = f32[8,128]{1,0:T(8,128)} copy(f32[8,128]{1,0:T(8,128)} %matern.1) | data formatting | bytes 8192

commit v3 on v2

v3 whole, which is shorter than its diff:
```python
import jax
import jax.numpy as jnp
from jax import lax
from jax.experimental import pallas as pl
from jax.experimental.pallas import tpu as pltpu
from jax.sharding import PartitionSpec as P

MESH = pl.DeviceIdType.MESH
F32, BF16 = jnp.float32, jnp.bfloat16

PTS = 128
FEAT = 128
RHS = 8
PLANES = 16
HALF = 8
HEAD = 2 * RHS
AUG = 16
COLS = 2 * PTS
RELAY = 6

SLOTS = (
    (0, 0), (1, 0), (0, 1), (1, 1), (1, -1), (-1, 0), (0, -1), (-1, -1), (-1, 1),
    (2, 0), (0, 2), (2, 2), (1, 2), (2, 1), (-1, 2), (2, -1),
)
PLACES = len(SLOTS)
NEAR = 9
LONE = (0, 9, 10, 11)
PASSED = ((11, 7, (-1, -1)), (15, 7, (-1, 0)), (14, 7, (0, -1)), (13, 3, (1, 0)), (12, 3, (0, 1)), (9, 1, (1, 0)), (10, 2, (0, 1)))
ROWS = PLACES * PTS
PART = NEAR * PTS
ENDS = (5 * PTS, 14 * PTS)


def packed(*tiles):
    return sum(tile * 9**i for i, tile in enumerate(tiles))


ORDERS = (packed(1, 2, 3, 4, 6, 5, 7, 8, 0), packed(1, 2, 6, 8, 7, 5, 3, 4, 0), packed(1, 2, 6, 5, 7, 8, 3, 4, 0))

SCALE = 5.0 / 3.0
ALPHA = 3.0 / 5.0**0.5
BETA = 0.6
DECAY = -(5.0**0.5) * 1.4426950408889634
TINY = 1e-30


def step_of(tile):
    return tile * (2 * ((tile + 3) // 8) - 1)


def split3(value):
    high = value.astype(BF16)
    rest = value - high.astype(F32)
    mid = rest.astype(BF16)
    low = (rest - mid.astype(F32)).astype(BF16)
    return high.astype(F32), mid.astype(F32), low.astype(F32)


def matern(dist2):
    r = dist2 * lax.rsqrt(dist2)
    return ((r + ALPHA) * r + BETA) * jnp.exp2(r * DECAY)


def kernel(
    feat_hbm, inv_hbm, vec_hbm, out_ref,
    feat_ref, inv_ref, vec_ref, abuf, bbuf, amat, va, rowacc, corr, work, mean, mid, wsum, colacc, cmsg, rmsg, rrecv, crecv,
    in_sem, plane_send, plane_recv, line_send, line_recv, sib_send, sib_recv, row_send, row_recv, col_send, col_recv,
):
    loads = [
        pltpu.make_async_copy(src, dst, in_sem.at[i])
        for i, (src, dst) in enumerate(((feat_hbm, feat_ref), (inv_hbm, inv_ref), (vec_hbm, vec_ref)))
    ]
    for load in loads:
        load.start()

    blk, wide = lax.axis_index("blk"), lax.axis_index("wide")
    core = lax.rem(blk, 2)
    x_here = 2 * lax.div(blk, HALF) + lax.div(wide, PLANES)
    y_here = lax.rem(lax.div(blk, 2), 4)
    plane = lax.rem(wide, PLANES)

    def device(dz, offset, other):
        x, y = lax.rem(x_here + offset[0] + 4, 4), lax.rem(y_here + offset[1] + 4, 4)
        z = lax.rem(plane + dz + PLANES, PLANES)
        c = 1 - core if other else core
        return {"blk": lax.div(x, 2) * HALF + y * 2 + c, "wide": lax.rem(x, 2) * PLANES + z}

    def back(offset):
        return (-offset[0], -offset[1])

    def plane_copy(k, source=0, offset=(0, 0)):
        return pltpu.make_async_remote_copy(
            src_ref=abuf.at[source], dst_ref=abuf.at[k], send_sem=plane_send.at[k], recv_sem=plane_recv.at[k],
            device_id=device(0, offset, False), device_id_type=MESH,
        )

    def pass_on(source):
        for k, at, offset in PASSED:
            if at == source:
                plane_copy(k, source, back(offset)).start()

    def line_copy(tile, source=0, hops=0):
        return pltpu.make_async_remote_copy(
            src_ref=bbuf.at[source, : HEAD + FEAT, :PTS], dst_ref=bbuf.at[tile, : HEAD + FEAT, :PTS],
            send_sem=line_send.at[tile], recv_sem=line_recv.at[tile],
            device_id=device(hops, (0, 0), False), device_id_type=MESH,
        )

    def sib_copy(tile):
        return pltpu.make_async_remote_copy(
            src_ref=bbuf.at[tile, : HEAD + FEAT, :PTS], dst_ref=bbuf.at[tile, : HEAD + FEAT, PTS:],
            send_sem=sib_send.at[tile], recv_sem=sib_recv.at[tile],
            device_id=device(0, (0, 0), True), device_id_type=MESH,
        )

    def row_copy(k):
        return pltpu.make_async_remote_copy(
            src_ref=rmsg.at[k], dst_ref=rrecv.at[k], send_sem=row_send.at[k], recv_sem=row_recv.at[k],
            device_id=device(0, SLOTS[k], False), device_id_type=MESH,
        )

    def col_copy(tile, other):
        return pltpu.make_async_remote_copy(
            src_ref=cmsg.at[tile, other], dst_ref=crecv.at[tile, other],
            send_sem=col_send.at[tile, other], recv_sem=col_recv.at[tile, other],
            device_id=device(step_of(tile), (0, 0), other == 1), device_id_type=MESH,
        )

    barrier = pltpu.get_barrier_semaphore()
    for dz in (RELAY, 2, -2, 1, -1):
        pl.semaphore_signal(barrier, inc=1, device_id=device(dz, (0, 0), False), device_id_type=MESH)
    for k in range(1, NEAR):
        pl.semaphore_signal(barrier, inc=1, device_id=device(0, SLOTS[k], False), device_id_type=MESH)
    pl.semaphore_signal(barrier, inc=1, device_id=device(0, (0, 0), True), device_id_type=MESH)

    for load in loads:
        load.wait()
    scaled = (feat_ref[...] * inv_ref[...]).astype(BF16).astype(F32)
    vec = vec_ref[...]
    vec_high = vec.astype(BF16).astype(F32)
    head = jnp.concatenate([vec_high, vec - vec_high], axis=0).astype(BF16)
    abuf[0, :PTS, :] = (scaled * -2.0).astype(BF16)
    abuf[0, PTS:, :] = head
    bbuf[0, :HEAD, :PTS] = head
    bbuf[0, HEAD : HEAD + FEAT, :PTS] = scaled.T.astype(BF16)

    pl.semaphore_wait(barrier, NEAR - 1 + 5 + 1)

    line_copy(RELAY, 0, -RELAY).start()
    line_copy(2, 0, 2).start()
    for k in (7, 3, 1, 2):
        plane_copy(k, 0, back(SLOTS[k])).start()
    line_copy(1, 0, 1).start()
    sib_copy(0).start()
    for k in (4, 5, 6, 8):
        plane_copy(k, 0, back(SLOTS[k])).start()

    lane = lax.broadcasted_iota(jnp.int32, (PTS, PTS), 1)
    ones = jnp.ones((2 * FEAT, PTS), BF16)

    def add_rows(k):
        at = k * PTS
        points = abuf[k, :PTS, :]
        wide_points = points.astype(F32)
        square = wide_points * wide_points
        high = square.astype(BF16)
        low = (square - high.astype(F32)).astype(BF16)
        norm = 0.25 * jnp.dot(jnp.concatenate([high, low], axis=1), ones, preferred_element_type=F32)
        n0, n1, n2 = split3(norm)
        extra = jnp.where(lane == 0, n0, jnp.where(lane == 1, n1, jnp.where(lane == 2, n2, jnp.where(lane < 6, 1.0, 0.0))))
        amat[at : at + PTS, :FEAT] = points
        amat[at : at + PTS, FEAT:] = extra.astype(BF16)
        va[0, :, at : at + PTS] = abuf[k, PTS:, :]

    def fetch(tile):
        line_copy(tile).wait_recv()
        sib_copy(tile).start()

    add_rows(0)
    rowacc[...] = jnp.zeros_like(rowacc)
    corr[...] = jnp.zeros_like(corr)
    for k in (7, 3, 1, 2):
        plane_copy(k).wait_recv()
        pass_on(k)
    for k in (7, 3, 1, 2):
        add_rows(k)
    fetch(1)
    fetch(2)
    line_copy(4, 2, 2).start()
    line_copy(3, 2, 1).start()
    for k in (4, 5, 6, 8):
        plane_copy(k).wait_recv()
    for k in (4, 5, 6, 8):
        add_rows(k)

    def both(value):
        return value[:RHS] + value[RHS:]

    def spread(value):
        return jnp.broadcast_to(jnp.sum(both(value), axis=1, keepdims=True), (RHS, COLS))

    wsum[0] = spread(va[0, :, :PART].astype(F32))
    mean[...] = jnp.dot(jnp.full((HEAD, PART), 1.0 / PART, BF16), amat[:PART], preferred_element_type=F32).astype(BF16)

    sub = lax.broadcasted_iota(jnp.int32, (AUG, COLS), 0)

    def add_columns(tile):
        cols = bbuf[tile, HEAD : HEAD + FEAT, :].astype(F32)
        n0, n1, n2 = split3(jnp.sum(cols * cols, axis=0, keepdims=True))
        extra = jnp.where(sub < 3, 1.0, jnp.where(sub == 3, n0, jnp.where(sub == 4, n1, jnp.where(sub == 5, n2, 0.0))))
        bbuf[tile, HEAD + FEAT :, :] = extra.astype(BF16)
        mid[tile] = matern(jnp.maximum(jnp.dot(mean[:, : FEAT + AUG], bbuf[tile, HEAD:, :], preferred_element_type=F32)[:RHS], TINY))

    def run_part(tile, first, last, kind):
        right = bbuf[tile, HEAD:, :]
        dist2 = jnp.dot(amat[first:last, : FEAT + AUG], right, preferred_element_type=F32)
        work[first:last] = jnp.maximum(dist2, TINY)
        entry = matern(work[first:last]).reshape((last - first) // RHS, RHS, COLS) - mid[tile][None]
        entry = entry.reshape(last - first, COLS).astype(BF16)
        rowacc[:, first:last] += lax.dot_general(
            bbuf[tile, :HEAD, :], entry, (((1,), (1,)), ((), ())), preferred_element_type=F32
        )
        return both(jnp.dot(va[kind, :, first:last], entry, preferred_element_type=F32))

    def add_constant(tile, *parts):
        constant = both(bbuf[tile, :HEAD, :].astype(F32)) * mid[tile]
        for part in parts:
            corr[part] += constant

    def first_part(tile):
        add_columns(tile)
        add_constant(tile, 0, 1, 2, 3)
        colacc[tile] = run_part(tile, 0, PART, 0) + wsum[0] * mid[tile]

    def second_part(tile):
        colacc[tile] += run_part(tile, PART, ROWS, 0) + wsum[1] * mid[tile]

    def whole_tile(tile):
        add_columns(tile)
        add_constant(tile, 0, 1, 2, 3)
        colacc[tile] = run_part(tile, 0, ROWS, 0) + (wsum[0] + wsum[1]) * mid[tile]

    def end_tile(tile):
        add_columns(tile)
        add_constant(tile, 0, 2)
        col = run_part(tile, 0, ENDS[0], 1) + run_part(tile, PART, ENDS[1], 1)
        colacc[tile] = col + wsum[2] * mid[tile]

    def send_columns(tile):
        total = colacc[tile]
        cmsg[tile, 0] = total[:, :PTS]
        cmsg[tile, 1] = total[:, PTS:]
        col_copy(tile, 0).start()
        col_copy(tile, 1).start()

    def early(tile, _):
        @pl.when((tile > 1) & (tile < 4))
        def _():
            fetch(tile + 1)

        @pl.when(tile == 4)
        def _():
            fetch(RELAY)
            line_copy(8, RELAY, -2).start()
            line_copy(7, RELAY, -1).start()
            line_copy(5, RELAY, 1).start()

        sib_copy(tile).wait_recv()
        first_part(tile)
        return 0

    lax.fori_loop(1, 5, early, 0)

    for k in range(NEAR, PLACES):
        plane_copy(k).wait_recv()
    for k in range(NEAR, PLACES):
        add_rows(k)
    wsum[1] = spread(va[0, :, PART:].astype(F32))
    k_of = lax.div(lax.broadcasted_iota(jnp.int32, (HEAD, ROWS), 1), PTS)
    once = k_of * PTS < ENDS[0]
    once = once | ((k_of >= NEAR) & (k_of * PTS < ENDS[1]))
    for k in LONE:
        once = once & (k_of != k)
    masked = jnp.where(once, va[0].astype(F32), 0.0)
    va[1] = masked.astype(BF16)
    wsum[2] = spread(masked)

    def late(index, order):
        tile = lax.rem(order, 9)
        order = order // 9
        after = lax.rem(order, 9)

        @pl.when((after == 5) | (after > RELAY))
        def _():
            fetch(after)

        @pl.when((tile == 0) | (tile > 4))
        def _():
            sib_copy(tile).wait_recv()

        @pl.when((tile == 0) | (tile == HALF))
        def _():
            end_tile(tile)

        @pl.when((tile > 4) & (tile < HALF))
        def _():
            whole_tile(tile)

        @pl.when((tile > 0) & (tile < 5))
        def _():
            second_part(tile)

        @pl.when(tile > 0)
        def _():
            send_columns(tile)

        return order

    third, quarter = lax.div(plane, 8), lax.div(plane, 12)
    order = ORDERS[0] + third * (ORDERS[1] - ORDERS[0]) + quarter * (ORDERS[2] - ORDERS[1])
    lax.fori_loop(0, HALF + 1, late, order)

    for k in range(PLACES):
        part = 2 * (k >= NEAR) + (k * PTS >= ENDS[0] if k < NEAR else k * PTS >= ENDS[1])
        rmsg[k] = both(rowacc[:, k * PTS : (k + 1) * PTS]) + jnp.sum(corr[part], axis=1, keepdims=True)
        if k:
            row_copy(k).start()
    cmsg[0, 1] = colacc[0, :, PTS:]
    col_copy(0, 1).start()

    total = rmsg[0] + colacc[0, :, :PTS]
    for tile in range(HALF + 1):
        for other in range(2):
            if tile or other:
                col_copy(tile, other).wait_recv()
                total += crecv[tile, other]
    for k in range(1, PLACES):
        row_copy(k).wait_recv()
        total += rrecv[k]
    out_ref[...] = total * SCALE

    for tile in range(HALF + 1):
        sib_copy(tile).wait_send()
        if tile:
            line_copy(tile).wait_send()
            col_copy(tile, 0).wait_send()
        col_copy(tile, 1).wait_send()
    for k in range(1, PLACES):
        plane_copy(k).wait_send()
        row_copy(k).wait_send()


def body(features, inv_length, vectors):
    dma = pltpu.SemaphoreType.DMA
    return pl.pallas_call(
        kernel,
        out_shape=jax.ShapeDtypeStruct((RHS, PTS), F32),
        in_specs=[pl.BlockSpec(memory_space=pltpu.HBM)] * 3,
        out_specs=pl.BlockSpec(memory_space=pltpu.VMEM),
        scratch_shapes=[
            pltpu.VMEM((PTS, FEAT), F32),
            pltpu.VMEM((1, FEAT), F32),
            pltpu.VMEM((RHS, PTS), F32),
            pltpu.VMEM((PLACES, PTS + HEAD, FEAT), BF16),
            pltpu.VMEM((HALF + 1, HEAD + FEAT + AUG, COLS), BF16),
            pltpu.VMEM((ROWS, 2 * FEAT), BF16),
            pltpu.VMEM((2, HEAD, ROWS), BF16),
            pltpu.VMEM((HEAD, ROWS), F32),
            pltpu.VMEM((4, RHS, COLS), F32),
            pltpu.VMEM((ROWS, COLS), F32),
            pltpu.VMEM((HEAD, 2 * FEAT), BF16),
            pltpu.VMEM((HALF + 1, RHS, COLS), F32),
            pltpu.VMEM((3, RHS, COLS), F32),
            pltpu.VMEM((HALF + 1, RHS, COLS), F32),
            pltpu.VMEM((HALF + 1, 2, RHS, PTS), F32),
            pltpu.VMEM((PLACES, RHS, PTS), F32),
            pltpu.VMEM((PLACES, RHS, PTS), F32),
            pltpu.VMEM((HALF + 1, 2, RHS, PTS), F32),
            dma((3,)),
            dma((PLACES,)), dma((PLACES,)),
            dma((HALF + 1,)), dma((HALF + 1,)),
            dma((HALF + 1,)), dma((HALF + 1,)),
            dma((PLACES,)), dma((PLACES,)),
            dma((HALF + 1, 2)), dma((HALF + 1, 2)),
        ],
        compiler_params=pltpu.CompilerParams(
            collective_id=0, has_side_effects=True, vmem_limit_bytes=60 * 2**20
        ),
        name="matern",
    )(features, inv_length.reshape(1, FEAT), vectors)


def solution(mesh):
    return jax.shard_map(
        body,
        mesh=mesh,
        in_specs=(P(("blk", "wide"), None), P(), P(None, ("blk", "wide"))),
        out_specs=P(None, ("blk", "wide")),
        check_vma=False,
    )
```

time: 45 us -> 44.3 us (0.984)
  Pallas kernels: 43.5 us -> 42.8 us
    pallas_call x1, Pallas kernels: 43.5 us -> 42.8 us  [body(): pl.pallas_call(kernel, out_shape=jax.ShapeDtypeStruct((RHS, PTS), F32), i...]
where the time goes in v3:
time: 44.3 us; the launch traced here: 44.1 us
  Pallas kernels  42.8 us (97%)
  local copies, waits for them, and re-layouts  1.28 us (3%)
    pallas_call x1, Pallas kernels, body(): pl.pallas_call(kernel, out_shape=jax.ShapeDtypeStruct((RHS, PTS), F32), i...  42.8 us
    unnamed x1, local copies, waits for them, and re-layouts  1.28 us

profile of v3, /device:TPU:1, one launch (start us, length us, event | category | flops | bytes accessed | tf_op | source)
XLA Modules:
  0.0 44.1 jit_solution(6514286731699204815)
XLA Ops:
  0.0 42.8 %matern.1 = f32[8,128]{1,0:T(8,128)} custom-call(f32[128,128]{1,0:T(8,128)} %feat_hbm.1, f32[1,128]{1,0:T(1,128)} %bitcast.1, f32[8,128]{1,0:T(8,128)} %vec_hbm.1), custom_call_target="tpu_custom_call" | custom-call | tf_op jit(solution)/shard_map/matern/pallas_call | solution.py:355
  42.8 1.3 %copy.5 = f32[8,128]{1,0:T(8,128)} copy(f32[8,128]{1,0:T(8,128)} %matern.1) | data formatting | bytes 8192

commit v4 on v3

--- a/solution.py
+++ b/solution.py
@@ -101,14 +101,14 @@
 
     def line_copy(tile, source=0, hops=0):
         return pltpu.make_async_remote_copy(
-            src_ref=bbuf.at[source, : HEAD + FEAT, :PTS], dst_ref=bbuf.at[tile, : HEAD + FEAT, :PTS],
+            src_ref=bbuf.at[source, :, :PTS], dst_ref=bbuf.at[tile, :, :PTS],
             send_sem=line_send.at[tile], recv_sem=line_recv.at[tile],
             device_id=device(hops, (0, 0), False), device_id_type=MESH,
         )
 
     def sib_copy(tile):
         return pltpu.make_async_remote_copy(
-            src_ref=bbuf.at[tile, : HEAD + FEAT, :PTS], dst_ref=bbuf.at[tile, : HEAD + FEAT, PTS:],
+            src_ref=bbuf.at[tile, :, :PTS], dst_ref=bbuf.at[tile, :, PTS:],
             send_sem=sib_send.at[tile], recv_sem=sib_recv.at[tile],
             device_id=device(0, (0, 0), True), device_id_type=MESH,
         )
@@ -142,7 +142,12 @@
     abuf[0, :PTS, :] = (scaled * -2.0).astype(BF16)
     abuf[0, PTS:, :] = head
     bbuf[0, :HEAD, :PTS] = head
-    bbuf[0, HEAD : HEAD + FEAT, :PTS] = scaled.T.astype(BF16)
+    turned = scaled.T
+    bbuf[0, HEAD : HEAD + FEAT, :PTS] = turned.astype(BF16)
+    n0, n1, n2 = split3(jnp.sum(turned * turned, axis=0, keepdims=True))
+    sub = lax.broadcasted_iota(jnp.int32, (AUG, PTS), 0)
+    extra = jnp.where(sub < 3, 1.0, jnp.where(sub == 3, n0, jnp.where(sub == 4, n1, jnp.where(sub == 5, n2, 0.0))))
+    bbuf[0, HEAD + FEAT :, :PTS] = extra.astype(BF16)
 
     pl.semaphore_wait(barrier, NEAR - 1 + 5 + 1)
 
@@ -202,13 +207,7 @@
     wsum[0] = spread(va[0, :, :PART].astype(F32))
     mean[...] = jnp.dot(jnp.full((HEAD, PART), 1.0 / PART, BF16), amat[:PART], preferred_element_type=F32).astype(BF16)
 
-    sub = lax.broadcasted_iota(jnp.int32, (AUG, COLS), 0)
-
     def add_columns(tile):
-        cols = bbuf[tile, HEAD : HEAD + FEAT, :].astype(F32)
-        n0, n1, n2 = split3(jnp.sum(cols * cols, axis=0, keepdims=True))
-        extra = jnp.where(sub < 3, 1.0, jnp.where(sub == 3, n0, jnp.where(sub == 4, n1, jnp.where(sub == 5, n2, 0.0))))
-        bbuf[tile, HEAD + FEAT :, :] = extra.astype(BF16)
         mid[tile] = matern(jnp.maximum(jnp.dot(mean[:, : FEAT + AUG], bbuf[tile, HEAD:, :], preferred_element_type=F32)[:RHS], TINY))
 
     def run_part(tile, first, last, kind):

time: 44.3 us -> 44.2 us (level)
  no operation moved by 1% of the time
where the time goes in v4:
time: 44.2 us; the launch traced here: 44 us
  Pallas kernels  42.8 us (97%)
  local copies, waits for them, and re-layouts  1.28 us (3%)
    pallas_call x1, Pallas kernels, body(): pl.pallas_call(kernel, out_shape=jax.ShapeDtypeStruct((RHS, PTS), F32), i...  42.8 us
    unnamed x1, local copies, waits for them, and re-layouts  1.28 us

profile of v4, /device:TPU:1, one launch (start us, length us, event | category | flops | bytes accessed | tf_op | source)
XLA Modules:
  0.0 44.0 jit_solution(2480970164949026537)
XLA Ops:
  0.0 42.8 %matern.1 = f32[8,128]{1,0:T(8,128)} custom-call(f32[128,128]{1,0:T(8,128)} %feat_hbm.1, f32[1,128]{1,0:T(1,128)} %bitcast.1, f32[8,128]{1,0:T(8,128)} %vec_hbm.1), custom_call_target="tpu_custom_call" | custom-call | tf_op jit(solution)/shard_map/matern/pallas_call | solution.py:354
  42.8 1.3 %copy.5 = f32[8,128]{1,0:T(8,128)} copy(f32[8,128]{1,0:T(8,128)} %matern.1) | data formatting | bytes 8192
